TPU v7x, 1024 devices: a whole 4x4x32 slice. The times are simulated.
1024 devices in a mesh: grp: 32 (over z), rep: 32 (over y, x, core).
Axes of the slice: x: 4, y: 4, z: 32, core: 2. Of those that a mesh axis runs over, the one named last changes fastest.
Arguments:
- item_factors: float32 [16384, 256], P('grp')
- light_factors: float32 [16384, 256], P(('grp', 'rep')), may hold values from -3 to 3
- heavy_factors: float32 [1024, 256], P('grp'), may hold values from -3 to 3
- requests: int32 [32768, 16], P(('grp', 'rep')), may hold values from 0 to 511
- counts: int32 [1024, 32], P(('grp', 'rep')), may hold values from 1 to 16, as said below
- slots: int32 [4194304], P(('grp', 'rep')), may hold values from 0 to 511
- confidence: float32 [4194304], P(('grp', 'rep')), may hold values from 1 to 10
- block_user: int32 [32768], P(('grp', 'rep')), may hold values from 0 to 47, as said below
- column_block: int32 [1], replicated, may hold values from 0 to 3
Outputs:
- light_new: float32 [16384, 256], P(('grp', 'rep'))
- heavy_new: float32 [1024, 256], P(('grp', 'rep'))
Inputs may be any that keep to these rules, and one draw needn't show every extreme that they name: `counts`: each count lies in 1 to 16; in every group one owner receives 16 live requests from every device of the group. `block_user`: values below 16 name the device's own light users, each of which has a block; 16 + h names heavy user h of the device's group.
All inputs are finite; a program needn't handle non-finite values.
Results may differ from a plain program's by a relative error of at most 0.0003.
Values sent between devices are 32-bit elements; how exact they have to be, the bound alone decides.
A program may use at most 32 MiB of HBM per device.

v0:
```python
import jax
import jax.numpy as jnp
from jax import lax
from jax.sharding import PartitionSpec as P

BLOCK_COLS = 64


unobserved = 128.0
ridge_weight = 1.0


def refine(factor_rows, normal, right, item_gram, column_start, prior_weight):
    gram_cols = lax.dynamic_slice_in_dim(item_gram, column_start, BLOCK_COLS, 1)
    gram_block = lax.dynamic_slice_in_dim(gram_cols, column_start, BLOCK_COLS, 0)
    old_block = lax.dynamic_slice_in_dim(factor_rows, column_start, BLOCK_COLS, 1)
    gram_user = jnp.dot(
        factor_rows, gram_cols, preferred_element_type=jnp.float32, precision=lax.Precision.HIGHEST
    )
    system = (
        normal + prior_weight * gram_block + ridge_weight * jnp.eye(BLOCK_COLS, dtype=normal.dtype)
    )
    right_side = right - prior_weight * gram_user - ridge_weight * old_block
    factor = jnp.linalg.cholesky(system)
    middle = lax.linalg.triangular_solve(factor, right_side[..., None], left_side=True, lower=True)
    update = lax.linalg.triangular_solve(
        factor, middle, left_side=True, lower=True, transpose_a=True
    )[..., 0]
    return lax.dynamic_update_slice_in_dim(factor_rows, old_block + update, column_start, 1)


def local(
    item_factors,
    light_factors,
    heavy_factors,
    requests,
    counts,
    slots,
    confidence,
    block_user,
    column_block,
):
    rank_width = item_factors.shape[1]
    groups = lax.axis_size("grp")
    helpers = lax.axis_size("rep")
    light_count = light_factors.shape[0]
    heavy_own = heavy_factors.shape[0] // helpers
    capacity = requests.shape[1]
    block_count = block_user.shape[0]
    block_rows = slots.shape[0] // block_count
    column_start = column_block[0] * BLOCK_COLS
    looked = jnp.take(
        item_factors,
        lax.all_to_all(requests, "grp", split_axis=0, concat_axis=0, tiled=True),
        axis=0,
    )
    fetched = lax.all_to_all(looked, "grp", split_axis=0, concat_axis=0, tiled=True)
    local_gram = jnp.dot(
        item_factors.T,
        item_factors,
        preferred_element_type=jnp.float32,
        precision=lax.Precision.HIGHEST,
    )
    item_gram = lax.psum(local_gram, "grp")
    fetched_flat = fetched.reshape(groups * capacity, rank_width)
    user_rows = jnp.concatenate([light_factors, heavy_factors], 0)
    score_table = jnp.einsum("uk,sk->us", user_rows, fetched_flat, precision=lax.Precision.HIGHEST)
    row_owner = jnp.repeat(block_user, block_rows)
    predicted = score_table[row_owner, slots]
    peer_match = (slots // capacity)[:, None] == jnp.arange(groups, dtype=jnp.int32)[None, :]
    live_limit = jnp.sum(jnp.where(peer_match, counts[0][None, :], 0), axis=1)
    weight = confidence * (slots % capacity < live_limit).astype(jnp.float32)
    block_columns = lax.dynamic_slice_in_dim(fetched_flat, column_start, BLOCK_COLS, 1)
    item_block = jnp.take(block_columns, slots, axis=0).reshape(block_count, block_rows, BLOCK_COLS)
    weight_blocks = weight.reshape(block_count, block_rows)
    residual = (weight * (1.0 - predicted)).reshape(block_count, block_rows)
    block_normal = jnp.einsum(
        "nrk,nrl->nkl",
        item_block * weight_blocks[..., None],
        item_block,
        precision=lax.Precision.HIGHEST,
    )
    block_right = jnp.einsum("nr,nrk->nk", residual, item_block, precision=lax.Precision.HIGHEST)
    onehot = (
        block_user[:, None] == jnp.arange(user_rows.shape[0], dtype=jnp.int32)[None, :]
    ).astype(jnp.float32)
    user_normal = jnp.einsum(
        "nu,nx->ux", onehot, block_normal.reshape(block_count, -1), precision=lax.Precision.HIGHEST
    ).reshape(-1, BLOCK_COLS, BLOCK_COLS)
    user_right = jnp.einsum("nu,nk->uk", onehot, block_right, precision=lax.Precision.HIGHEST)
    heavy_normal = user_normal[light_count:]
    heavy_right = user_right[light_count:]
    first_heavy = lax.axis_index("rep") * heavy_own
    total_normal, total_right = lax.psum((heavy_normal, heavy_right), "rep")
    own_normal = lax.dynamic_slice_in_dim(total_normal, first_heavy, heavy_own, 0)
    own_right = lax.dynamic_slice_in_dim(total_right, first_heavy, heavy_own, 0)
    own_factors = lax.dynamic_slice_in_dim(heavy_factors, first_heavy, heavy_own, 0)
    item_total = item_factors.shape[0] * groups
    all_rows = jnp.concatenate([light_factors, own_factors], 0)
    all_normal = jnp.concatenate([user_normal[:light_count], own_normal], 0)
    all_right = jnp.concatenate([user_right[:light_count], own_right], 0)
    updated = refine(
        all_rows, all_normal, all_right, item_gram, column_start, unobserved / item_total
    )
    return (updated[:light_count], updated[light_count:])


def solution(mesh):
    return jax.shard_map(
        local,
        mesh=mesh,
        in_specs=(
            P("grp", None),
            P(("grp", "rep"), None),
            P("grp", None),
            P(("grp", "rep"), None),
            P(("grp", "rep"), None),
            P(("grp", "rep")),
            P(("grp", "rep")),
            P(("grp", "rep")),
            P(),
        ),
        out_specs=(P(("grp", "rep"), None), P(("grp", "rep"), None)),
        check_vma=False,
    )
```

profile of v0, /device:TPU:1, one launch (start us, length us, event | category | flops | bytes accessed | tf_op | source)
XLA Modules:
  0.0 758.5 jit_solution(12901153076575835194)
XLA Ops:
  8.0 0.8 copy.31
  8.8 50.3 %all_to_all.20 = s32[32,1,16]{2,1,0:T(1,128)S(1)} all-to-all(s32[32,1,16]{2,1,0:T(1,128)S(1)} %bitcast.59), channel_id=1, replica_groups=mesh['grp'=32,'rep'=32] {'grp'}, dimensions={0} | all-to-all | bytes 4096 | tf_op jit(solution)/shard_map/all_to_all | solution.py:54
  59.2 0.1 reshape.134
  59.3 1.6 gather_fusion
  60.9 0.9 broadcast_select_fusion
  61.9 3.9 all-to-all-start.1
  65.8 0.0 all-reduce.5.cloned.1.call-start
  65.8 1.7 fusion.45
  67.5 0.0 all-reduce.3.cloned.1.call-start
  67.7 0.2 select_reduce_fusion.1
  67.9 0.1 broadcast_in_dim.63
  68.7 0.1 copy.36
  68.8 249.0 %all-reduce.5.cloned.1.call-done = f32[256,256]{1,0:T(8,128)} async-done(((f32[256,256]{1,0:T(8,128)}), f32[256,256]{1,0:T(8,128)}) %all-reduce.5.cloned.1.call-update) | async-done | bytes 262160 | tf_op jit(solution)/shard_map/psum | solution.py:64
  317.8 1.0 dynamic-slice_multiply_fusion
  318.7 0.1 copy.35
  318.8 0.6 fusion.20
  319.4 0.1 constant_dynamic-slice_fusion.2
  319.5 14.2 %gather_fusion.1 = f32[4096,64]{1,0:T(8,128)} fusion(f32[512,64]{1,0:T(8,128)S(1)} %constant_dynamic-slice_fusion.2, s32[4096]{0:T(1024)S(1)} %get-tuple-element.6), kind=kCustom, calls=%fused_computation.1 | custom fusion | bytes 2113536 | tf_op jit(solution)/shard_map/jit(_take)/gather | solution.py:74
  333.7 2.2 copy.32
  335.9 32.8 %gather_fusion.2 = f32[4096]{0:T(1024)S(1)} fusion(f32[48,512]{1,0:T(8,128)S(1)} %fusion.20, s32[4096]{0:T(1024)S(1)} %bitcast.48), kind=kCustom, calls=%fused_computation.2 | custom fusion | bytes 65536 | tf_op jit(solution)/shard_map/gather | solution.py:69
  368.7 1.7 fusion.6
  370.4 1.8 fusion
  372.3 0.4 reshape.129
  372.6 0.6 fusion.29
  373.3 0.4 slice.41
  373.7 1.4 copy.33
  375.0 0.0 all-reduce.3.cloned.1.call-update
  375.1 0.3 fusion.28
  375.4 0.2 slice.39
  375.6 0.2 copy.34
  375.8 138.6 %psum.23 = f32[32,64]{1,0:T(8,128)S(1)} all-reduce(f32[32,64]{1,0:T(8,128)S(1)} %slice.55), channel_id=1, replica_groups=mesh['grp'=32,'rep'=32] {'rep'}, use_global_device_ids=true, to_apply=%region_5.6 | all-reduce | flops 2048 | bytes 16384 | tf_op jit(solution)/shard_map/psum | solution.py:94
  514.5 0.3 fusion.4
  514.7 48.5 %all-reduce.3.cloned.1.call-done = f32[32,64,64]{1,2,0:T(8,128)} async-done(((f32[32,64,64]{1,2,0:T(8,128)}), f32[32,64,64]{1,2,0:T(8,128)}) %all-reduce.3.cloned.1.call-update) | async-done | bytes 524304 | tf_op jit(solution)/shard_map/psum | solution.py:94
  563.2 0.8 constant_dynamic-slice_fusion.1
  564.0 0.1 fusion.8
  564.1 0.2 copy.37
  564.3 0.1 fusion.13
  564.4 99.6 %custom-call.9 = f32[17,64,64]{2,1,0:T(8,128)S(1)} custom-call(f32[17,64,64]{2,1,0:T(8,128)S(1)} %fusion.13), custom_call_target="Cholesky" | custom-call | tf_op jit(solution)/shard_map/jit(cholesky)/cholesky | solution.py:24
  664.0 0.1 select_reduce_fusion
  664.1 0.1 compare_reduce_fusion
  664.2 0.1 select_bitcast_fusion
  664.4 83.6 %custom-call.10 = f32[17,1,64,64]{2,3,1,0:T(8,128)S(1)} custom-call(f32[17,1,64,64]{3,2,1,0:T(8,128)S(1)} %select_bitcast_fusion), custom_call_target="InvertDiagBlocksLowerTriangular" | custom-call | tf_op jit(solution)/shard_map/triangular_solve | solution.py:26
  747.9 0.6 fusion.11
  748.5 1.0 fusion.9
  749.5 0.1 bitcast_add_fusion.1
  749.6 0.3 dynamic_update_slice.3
  749.9 0.6 slice.57
  750.5 0.6 slice.56
  (36 shorter events, 0.3 us)
Async XLA Ops:
  8.0 51.3 %copy-start = (f32[512,256]{1,0:T(8,128)S(1)}, f32[512,256]{1,0:T(8,128)}, u32[]{:S(2)}) copy-start(f32[512,256]{1,0:T(8,128)} %param.9) | copy-start | bytes 1572868
  60.9 6.7 copy-start.4
  60.9 6.8 copy-start.1
  60.9 6.8 copy-start.2
  60.9 6.8 copy-start.7
  60.9 7.0 copy-start.6
  61.9 256.9 %all-to-all-start.1 = ((f32[32,16,256]{2,1,0:T(8,128)}), f32[32,16,256]{2,1,0:T(8,128)S(1)}, u32[]{:S(2)}, u32[]{:S(2)}) async-start(f32[32,16,256]{2,1,0:T(8,128)} %broadcast_select_fusion), calls=%async_computation.1 | async-start | bytes 1048576 | tf_op jit(solution)/shard_map/all_to_all | solution.py:57
  65.8 252.0 %all-reduce.5.cloned.1.call-start = ((), (), s32[]{:S(2)}) async-start(), calls=%async_computation.3 | async-start | bytes 524288 | tf_op jit(solution)/shard_map/psum | solution.py:64
  67.5 495.7 %all-reduce.3.cloned.1.call-start = ((), (), s32[]{:S(2)}) async-start(), calls=%async_computation.2 | async-start | bytes 2097152 | tf_op jit(solution)/shard_map/psum | solution.py:94
  335.9 32.8 %copy-start.5 = (f32[4096]{0:T(1024)S(1)}, f32[4096]{0:T(1024)}, u32[]{:S(2)}) copy-start(f32[4096]{0:T(1024)} %param.15) | copy-start | bytes 49156
  375.0 139.4 %copy-start.3 = (f32[256,256]{1,0:T(8,128)S(1)}, f32[256,256]{1,0:T(8,128)}, u32[]{:S(2)}) copy-start(f32[256,256]{1,0:T(8,128)} %all-reduce.5.cloned.1.call-done) | copy-start | bytes 786436
Sparse Core Ops, SparseCore 0:
  69.0 248.7 all-reduce.4
Sparse Core Ops, SparseCore 1:
  375.2 188.0 all-reduce.2
where the time goes:
time: 759 us
  waiting for transfers between devices  298 us (39%)
  blocking collectives  189 us (25%)
  other arithmetic  186 us (25%)
  local copies, waits for them, and re-layouts  57.1 us (8%)
  between operations  16.5 us (2%)
  matrix products  8.56 us (1%)
    psum x1, waiting for transfers between devices, local(): item_gram = lax.psum(local_gram, 'grp')  249 us
    psum x1, blocking collectives, local(): total_normal, total_right = lax.psum((heavy_normal, heavy_right), 'rep')  139 us
    another operation x4, other arithmetic, refine(): factor = jnp.linalg.cholesky(system)  99.8 us
    another operation x3, other arithmetic, refine(): lax.linalg.triangular_solve(factor, middle, left_side=True, lower=True, t...  83.7 us
    all_to_all x1, blocking collectives, local(): lax.all_to_all(requests, 'grp', split_axis=0, concat_axis=0, tiled=True)  50.3 us
    psum x1, waiting for transfers between devices, local(): total_normal, total_right = lax.psum((heavy_normal, heavy_right), 'rep')  48.5 us
    gather x1, local copies, waits for them, and re-layouts, local(): predicted = score_table[row_owner, slots]  32.8 us
    gather x2, local copies, waits for them, and re-layouts, local(): jnp.take(block_columns, slots, axis=0)  16.3 us
  transfers between devices with their start and end apart: 3, of which 2 were waited for; matrix products, arithmetic and copies ran while one was open for 1% of the time, Pallas kernels for 0%

commit v1 on v0

v1 whole, which is shorter than its diff:
```python
import functools

import jax
import jax.numpy as jnp
from jax import lax
from jax.experimental import pallas as pl
from jax.experimental.pallas import tpu as pltpu
from jax.sharding import PartitionSpec as P

COLS = 64
RANK = 256
SLOTS = 512
CAP = 16
LIGHT = 16
HEAVY = 32
TILE = 8
PANELS = COLS // TILE
UNOBSERVED = 128.0
MESH = pl.DeviceIdType.MESH
F32 = jnp.float32
BF16 = jnp.bfloat16
HIGHEST = lax.Precision.HIGHEST
VMEM = pl.BlockSpec(memory_space=pltpu.VMEM)
SMEM = pl.BlockSpec(memory_space=pltpu.SMEM)
LIMIT = 48 * 1024 * 1024

WIDTH = [COLS - TILE * b for b in range(PANELS)]
START = [sum(TILE * w for w in WIDTH[:b]) for b in range(PANELS)]
ENTRIES = sum(TILE * w for w in WIDTH)
LINES = ENTRIES // 128
MESSAGE = 24


def iota(shape, dim):
    return lax.broadcasted_iota(jnp.int32, shape, dim)


def rows_by_rows(a, b, precision=HIGHEST):
    return lax.dot_general(a, b, (((1,), (1,)), ((), ())), precision=precision, preferred_element_type=F32)


def split(x, parts):
    out = []
    for _ in range(parts):
        part = x.astype(BF16)
        out.append(part)
        x = x - part.astype(F32)
    return out


def picker(column_block):
    return (iota((COLS, RANK), 1) == iota((COLS, RANK), 0) + column_block * COLS).astype(F32)


def exact_one_hot_dot(one_hot, x):
    hot = one_hot.astype(BF16)
    return sum(jnp.dot(hot, part, preferred_element_type=F32) for part in split(x, 3))


def fetch_kernel(
    n,
    items_total,
    cb_ref,
    user_ref,
    items_ref,
    req_ref,
    slots_ref,
    conf_ref,
    h_ref,
    gram_ref,
    c_ref,
    ring,
    owned,
    answer,
    ask_out,
    ask_in,
    part_out,
    part_in,
    sum_out,
    sum_in,
    weight_sum,
    right_s,
    right_r,
    left_s,
    left_r,
    own_s,
    own_r,
    ask_s,
    ask_r,
    ans_s,
    ans_r,
    part_s,
    part_r,
    sum_s,
    sum_r,
):
    g, r = lax.axis_index("grp"), lax.axis_index("rep")
    right, left = lax.rem(g + 1, n), lax.rem(g + n - 1, n)
    share = ring.shape[1]

    def put(src, dst, send, recv, target):
        return pltpu.make_async_remote_copy(
            src_ref=src, dst_ref=dst, send_sem=send, recv_sem=recv, device_id=target, device_id_type=MESH
        )

    def peers(body):
        def one(k, carry):
            body(lax.rem(r + k, n))
            return carry

        lax.fori_loop(1, n, one, 0)

    barrier = pltpu.get_barrier_semaphore()
    peers(lambda p: pl.semaphore_signal(barrier, inc=1, device_id=(g, p), device_id_type=MESH))
    pl.semaphore_signal(barrier, inc=1, device_id=(left, r), device_id_type=MESH)
    pl.semaphore_signal(barrier, inc=1, device_id=(right, r), device_id_type=MESH)
    ring[g] = items_ref[pl.ds(pl.multiple_of(r * share, share), share), :]
    spread = (
        (iota((CAP, 128), 1) % CAP == iota((CAP, 128), 0)) & (iota((CAP, 128), 1) // CAP == lax.rem(r, TILE))
    ).astype(F32)
    asked = jnp.dot(req_ref[...].astype(F32), spread, precision=HIGHEST, preferred_element_type=F32)
    for p in range(n):
        ask_out[p] = asked[p : p + 1, :]
    weight_sum[...] = jnp.zeros_like(weight_sum)
    pl.semaphore_wait(barrier, n + 1)

    def go_right(t):
        p = lax.rem(g + n - t, n)
        return put(ring.at[p], ring.at[p], right_s.at[t], right_r.at[t], (right, r))

    def go_left(t):
        p = lax.rem(g + t, n)
        return put(ring.at[p], ring.at[p], left_s.at[t], left_r.at[t], (left, r))

    def came_right(t):
        p = lax.rem(g + n - t - 1, n)
        put(ring.at[p], ring.at[p], right_s.at[t], right_r.at[t], (right, r)).wait_recv()
        return p

    def came_left(t):
        p = lax.rem(g + t + 1, n)
        put(ring.at[p], ring.at[p], left_s.at[t], left_r.at[t], (left, r)).wait_recv()
        return p

    def to_owner(p):
        return put(ring.at[p], owned.at[r], own_s.at[p], own_r.at[r], (g, p))

    def hand_over(p):
        @pl.when(p != r)
        def _():
            to_owner(p).start()

        @pl.when(p == r)
        def _():
            owned[r] = ring[p]

    def ask(p):
        return put(ask_out.at[p], ask_in.at[r], ask_s.at[p], ask_r.at[r], (g, p))

    def asked_by(p):
        return put(ask_out.at[p], ask_in.at[p], ask_s.at[p], ask_r.at[p], (g, p))

    def weigh(step):
        hot, parts = [], [[], [], []]
        for half in range(2):
            row = 2 * step + half
            slot = slots_ref[pl.ds(row, 1), :]
            hot.append((iota((SLOTS, 128), 0) == slot).astype(F32).astype(BF16))
            user = (iota((LIGHT + HEAVY, 128), 0) == user_ref[row]).astype(F32)
            for k, part in enumerate(split(conf_ref[pl.ds(row, 1), :], 3)):
                parts[k].append(user * part.astype(F32))
        lhs = jnp.concatenate([jnp.concatenate(p, 1) for p in parts], 0).astype(BF16)
        weight_sum[...] += rows_by_rows(lhs, jnp.concatenate(hot, 1), None)

    half = n // 2
    go_right(0).start()
    go_left(0).start()
    hand_over(g)
    peers(lambda p: ask(p).start())
    ask_in[r] = ask_out[r]

    def ring_step(t, carry):
        p = came_right(t - 1)
        go_right(t).start()
        q = came_left(t - 1)

        @pl.when(t < half - 1)
        def _():
            go_left(t).start()

        hand_over(p)
        hand_over(q)
        weigh(t - 1)
        return carry

    lax.fori_loop(1, half, ring_step, 0)
    hand_over(came_right(half - 1))
    weigh(half - 1)

    peers(lambda p: asked_by(p).wait_recv())
    lines = [jnp.sum(ask_in[TILE * q : TILE * q + TILE], axis=0) for q in range(n // TILE)]
    lines = jnp.concatenate(lines + [jnp.zeros((TILE - len(lines), 128), F32)], 0)
    eye = (iota((128, 128), 0) == iota((128, 128), 1)).astype(F32)
    wanted = rows_by_rows(eye, lines)
    hots = [(wanted[:, q : q + 1] == iota((128, SLOTS), 1).astype(F32)).astype(F32) for q in range(n // TILE)]

    def handed_by(p):
        return put(ring.at[p], owned.at[p], own_s.at[p], own_r.at[p], (g, p))

    def reply(p):
        return put(answer.at[p], h_ref.at[r], ans_s.at[p], ans_r.at[r], (g, p))

    def replied_by(p):
        return put(answer.at[p], h_ref.at[p], ans_s.at[p], ans_r.at[p], (g, p))

    peers(lambda p: handed_by(p).wait_recv())
    rows = owned[...].reshape(n * share, RANK)
    for q, hot in enumerate(hots):
        answer[TILE * q : TILE * q + TILE] = exact_one_hot_dot(hot, rows).reshape(TILE, CAP, RANK)
    peers(lambda p: reply(p).start())
    h_ref[r] = answer[r]

    mine = ring[...].reshape(n * share, RANK)
    pick = picker(cb_ref[0])
    mine_cols = rows_by_rows(pick, mine)
    part = jnp.dot(mine_cols, mine, precision=HIGHEST, preferred_element_type=F32)
    for k in range(n):
        a, b, c = k // 4, (k // 2) % 2, k % 2
        part_out[k] = part[8 * a + 4 * c : 8 * a + 4 * c + 4, 128 * b : 128 * b + 128]

    def give(p):
        return put(part_out.at[p], part_in.at[r], part_s.at[p], part_r.at[r], (g, p))

    def given_by(p):
        return put(part_out.at[p], part_in.at[p], part_s.at[p], part_r.at[p], (g, p))

    def share_sum(p):
        return put(sum_out.at[0], sum_in.at[r], sum_s.at[p], sum_r.at[r], (g, p))

    def sum_of(p):
        return put(sum_out.at[0], sum_in.at[p], sum_s.at[p], sum_r.at[p], (g, p))

    peers(lambda p: give(p).start())
    part_in[r] = part_out[r]
    peers(lambda p: given_by(p).wait_recv())
    sum_out[0] = jnp.sum(part_in[...], axis=0)
    peers(lambda p: share_sum(p).start())
    sum_in[r] = sum_out[0]
    users = LIGHT + HEAVY
    c_ref[...] = weight_sum[:users] + weight_sum[users : 2 * users] + weight_sum[2 * users :]
    peers(lambda p: sum_of(p).wait_recv())
    for k in range(n):
        a, b, c = k // 4, (k // 2) % 2, k % 2
        gram_ref[8 * a + 4 * c : 8 * a + 4 * c + 4, 128 * b : 128 * b + 128] = sum_in[k]
    peers(lambda p: replied_by(p).wait_recv())

    def sent_right(t, carry):
        go_right(t).wait_send()
        return carry

    def sent_left(t, carry):
        go_left(t).wait_send()
        return carry

    lax.fori_loop(0, half, sent_right, 0)
    lax.fori_loop(0, half - 1, sent_left, 0)
    for sent in (to_owner, ask, reply, give, share_sum):
        peers(lambda p, sent=sent: sent(p).wait_send())


def fetch(n, items, requests, slots, confidence, block_user, column_block):
    share = items.shape[0] // n
    dma = [pltpu.SemaphoreType.DMA((n,)) for _ in range(14)]
    users = LIGHT + HEAVY
    return pl.pallas_call(
        functools.partial(fetch_kernel, n, items.shape[0] * n),
        out_shape=(
            jax.ShapeDtypeStruct((n, CAP, RANK), F32),
            jax.ShapeDtypeStruct((COLS, RANK), F32),
            jax.ShapeDtypeStruct((users, SLOTS), F32),
        ),
        in_specs=[SMEM, SMEM, VMEM, VMEM, VMEM, VMEM],
        out_specs=(VMEM, VMEM, VMEM),
        scratch_shapes=[
            pltpu.VMEM((n, share, RANK), F32),
            pltpu.VMEM((n, share, RANK), F32),
            pltpu.VMEM((n, CAP, RANK), F32),
            pltpu.VMEM((n, 1, 128), F32),
            pltpu.VMEM((n, 1, 128), F32),
            pltpu.VMEM((n, 4, 128), F32),
            pltpu.VMEM((n, 4, 128), F32),
            pltpu.VMEM((1, 4, 128), F32),
            pltpu.VMEM((n, 4, 128), F32),
            pltpu.VMEM((3 * users, SLOTS), F32),
            *dma,
        ],
        compiler_params=pltpu.CompilerParams(collective_id=0, has_side_effects=True, vmem_limit_bytes=LIMIT),
        name="fetch",
    )(column_block, block_user, items, requests, slots, confidence)


def normal_kernel(cb_ref, h_ref, c_ref, counts_ref, light_ref, heavy_ref, flat_ref, right_ref, msg_ref):
    users = LIGHT + HEAVY
    rows = h_ref[...].reshape(SLOTS, RANK)
    owners = counts_ref.shape[1]
    by_slot = (iota((owners, SLOTS), 1) // CAP == iota((owners, SLOTS), 0)).astype(BF16)
    limit = jnp.dot(
        jnp.broadcast_to(counts_ref[...], (TILE, owners)).astype(F32).astype(BF16),
        by_slot,
        preferred_element_type=F32,
    )[:1]
    live = (iota((1, SLOTS), 1) % CAP).astype(F32) < limit
    weight = jnp.where(live, c_ref[...], 0.0)
    factors = jnp.concatenate([light_ref[...], heavy_ref[...]], 0)
    residual = weight * (1.0 - rows_by_rows(factors, rows))
    cols = rows_by_rows(picker(cb_ref[0]), rows)
    none = jnp.zeros((64 - users, SLOTS), F32)
    right = rows_by_rows(cols, jnp.concatenate([residual, jnp.zeros((128 - users, SLOTS), F32)], 0))
    right_ref[...] = right
    high, low = [part.astype(F32) for part in split(weight, 2)]
    both = jnp.concatenate([high, none, low, none], 0).astype(BF16)
    once = jnp.concatenate([high, none, jnp.zeros((64, SLOTS), F32)], 0).astype(BF16)
    for b in range(PANELS):
        width = WIDTH[b]
        tail = cols[TILE * b :]
        product = jnp.concatenate([tail * cols[TILE * b + i : TILE * b + i + 1] for i in range(TILE)], 0)
        p_high, p_low = split(product, 2)
        first = rows_by_rows(p_high, both, None)
        second = rows_by_rows(p_low, once, None)
        flat_ref[START[b] : START[b] + TILE * width, :] = first + pltpu.roll(first, 64, 1) + second
    for q in range(LINES):
        turned = flat_ref[128 * q : 128 * q + 128, :].T
        msg_ref[:, q, :] = turned[LIGHT:users]
    turned = jnp.concatenate([right, jnp.zeros((64, 128), F32)], 0).T
    msg_ref[:, LINES, :] = turned[LIGHT:users]
    for q in range(LINES + 1, MESSAGE):
        msg_ref[:, q, :] = jnp.zeros((HEAVY, 128), F32)


def normals(h, c, counts, light, heavy, column_block):
    return pl.pallas_call(
        normal_kernel,
        out_shape=(
            jax.ShapeDtypeStruct((ENTRIES, 128), F32),
            jax.ShapeDtypeStruct((COLS, 128), F32),
            jax.ShapeDtypeStruct((HEAVY, MESSAGE, 128), F32),
        ),
        in_specs=[SMEM, VMEM, VMEM, VMEM, VMEM, VMEM],
        out_specs=(VMEM, VMEM, VMEM),
        compiler_params=pltpu.CompilerParams(vmem_limit_bytes=LIMIT),
        name="normals",
    )(column_block, h, c, counts, light, heavy)


def reduce_kernel(n, msg_ref, out_ref, landed, send, recv):
    g, r = lax.axis_index("grp"), lax.axis_index("rep")

    def peers(body):
        def one(k, carry):
            body(lax.rem(r + k, n))
            return carry

        lax.fori_loop(1, n, one, 0)

    barrier = pltpu.get_barrier_semaphore()
    peers(lambda p: pl.semaphore_signal(barrier, inc=1, device_id=(g, p), device_id_type=MESH))
    pl.semaphore_wait(barrier, n - 1)

    def put(p, slot):
        return pltpu.make_async_remote_copy(
            src_ref=msg_ref.at[p],
            dst_ref=landed.at[slot],
            send_sem=send.at[p],
            recv_sem=recv.at[slot],
            device_id=(g, p),
            device_id_type=MESH,
        )

    peers(lambda p: put(p, r).start())
    landed[r] = msg_ref[r]
    peers(lambda p: put(p, p).wait_recv())
    out_ref[...] = jnp.sum(landed[...], axis=0)
    peers(lambda p: put(p, r).wait_send())


def reduce_heavy(n, message):
    return pl.pallas_call(
        functools.partial(reduce_kernel, n),
        out_shape=jax.ShapeDtypeStruct((MESSAGE, 128), F32),
        in_specs=[VMEM],
        out_specs=VMEM,
        scratch_shapes=[
            pltpu.VMEM((n, MESSAGE, 128), F32),
            pltpu.SemaphoreType.DMA((n,)),
            pltpu.SemaphoreType.DMA((n,)),
        ],
        compiler_params=pltpu.CompilerParams(collective_id=1, has_side_effects=True, vmem_limit_bytes=LIMIT),
        name="reduce_heavy",
    )(message)


def solve_kernel(
    prior,
    cb_ref,
    flat_ref,
    right_ref,
    heavy_sum_ref,
    gram_ref,
    light_ref,
    heavy_ref,
    light_out,
    heavy_out,
    a_ref,
    l_ref,
    inv_ref,
    x_ref,
):
    r = lax.axis_index("rep")
    pick = picker(cb_ref[0])
    own = heavy_ref[pl.ds(r, 1), :]
    factors = jnp.concatenate([light_ref[...], own, jnp.zeros((128 - LIGHT - 1, RANK), F32)], 0)
    gram = prior * gram_ref[...]
    block = rows_by_rows(gram, pick) + (iota((COLS, COLS), 0) == iota((COLS, COLS), 1)).astype(F32)
    pulled = rows_by_rows(gram + pick, factors)
    turned = jnp.concatenate([heavy_sum_ref[...], jnp.zeros((128 - MESSAGE, 128), F32)], 0).T
    lane = iota((1, 128), 1)
    is_light, is_heavy = lane < LIGHT, lane == LIGHT
    right = jnp.where(is_light, right_ref[...], jnp.where(is_heavy, turned[:COLS, LINES : LINES + 1], 0.0)) - pulled
    for q in range(LINES):
        part = flat_ref[128 * q : 128 * q + 128, :]
        flat_ref[128 * q : 128 * q + 128, :] = jnp.where(
            is_light, part, jnp.where(is_heavy, turned[:, q : q + 1], 0.0)
        )
    for i in range(COLS):
        b = i // TILE
        at = START[b] + (i - TILE * b) * WIDTH[b]
        a_ref[i, TILE * b : COLS, :] = flat_ref[at : at + WIDTH[b], :] + block[TILE * b :, i : i + 1]
        a_ref[i, COLS : COLS + TILE, :] = jnp.broadcast_to(right[i : i + 1, :], (TILE, 128))

    tiles = PANELS + 1
    for b in range(PANELS):
        base = TILE * b
        acc = {
            (k, t): a_ref[base + k, TILE * t : TILE * t + TILE, :] for k in range(TILE) for t in range(b, tiles)
        }
        for k in range(TILE):
            own_tile = acc[k, b]
            inv = 1.0 / jnp.broadcast_to(own_tile[k : k + 1], (TILE, 128))
            inv_ref[base + k] = inv
            for t in range(b, tiles):
                if t > b:
                    a_ref[base + k, TILE * t : TILE * t + TILE, :] = acc[k, t]
                    if t < PANELS:
                        l_ref[base + k, TILE * t : TILE * t + TILE, :] = acc[k, t] * inv
            a_ref[base + k, base : base + TILE, :] = own_tile
            for k2 in range(k + 1, TILE):
                factor = jnp.broadcast_to(own_tile[k2 : k2 + 1], (TILE, 128)) * inv
                for t in range(b, tiles):
                    acc[k2, t] = acc[k2, t] - factor * acc[k, t]
        for s in range(b + 1, PANELS):
            for k2 in range(TILE):
                row = TILE * s + k2
                factors_ = [
                    jnp.broadcast_to(l_ref[base + k, row : row + 1, :], (TILE, 128)) for k in range(TILE)
                ]
                for t in range(s, tiles):
                    total = a_ref[row, TILE * t : TILE * t + TILE, :]
                    for k in range(TILE):
                        total = total - factors_[k] * a_ref[base + k, TILE * t : TILE * t + TILE, :]
                    a_ref[row, TILE * t : TILE * t + TILE, :] = total

    x = [None] * PANELS
    place = iota((TILE, 128), 0)
    for b in reversed(range(PANELS)):
        base = TILE * b
        left = []
        for k in range(TILE):
            value = a_ref[base + k, COLS : COLS + TILE, :]
            if b + 1 < PANELS:
                total = sum(
                    a_ref[base + k, TILE * t : TILE * t + TILE, :] * x[t] for t in range(b + 1, PANELS)
                )
                value = value - jnp.sum(total, axis=0, keepdims=True)
            left.append(value)
        found = jnp.zeros((TILE, 128), F32)
        for k in reversed(range(TILE)):
            value = left[k] * inv_ref[base + k]
            found = jnp.where(place == k, value, found)
            for k2 in range(k):
                left[k2] = left[k2] - jnp.broadcast_to(a_ref[base + k2, base + k : base + k + 1, :], (TILE, 128)) * value
        x[b] = found
        x_ref[base : base + TILE, :] = found
    x_ref[COLS:, :] = jnp.zeros((128 - COLS, 128), F32)
    delta = x_ref[...].T[:, :COLS]
    delta = jnp.concatenate([delta, delta, delta, delta], 1)
    inside = iota((1, RANK), 1) // COLS == cb_ref[0]
    light_out[...] = light_ref[...] + jnp.where(inside, delta[:LIGHT], 0.0)
    heavy_out[...] = own + jnp.where(inside, delta[LIGHT : LIGHT + 1], 0.0)


def solve(prior, flat, right, heavy_sum, gram, light, heavy, column_block):
    return pl.pallas_call(
        functools.partial(solve_kernel, prior),
        out_shape=(jax.ShapeDtypeStruct((LIGHT, RANK), F32), jax.ShapeDtypeStruct((1, RANK), F32)),
        in_specs=[SMEM, VMEM, VMEM, VMEM, VMEM, VMEM, VMEM],
        out_specs=(VMEM, VMEM),
        scratch_shapes=[
            pltpu.VMEM((COLS, COLS + TILE, 128), F32),
            pltpu.VMEM((COLS, COLS, 128), F32),
            pltpu.VMEM((COLS, TILE, 128), F32),
            pltpu.VMEM((128, 128), F32),
        ],
        compiler_params=pltpu.CompilerParams(vmem_limit_bytes=LIMIT),
        name="solve",
    )(column_block, flat, right, heavy_sum, gram, light, heavy)


def local(items, light, heavy, requests, counts, slots, confidence, block_user, column_block):
    n = lax.axis_size("grp")
    blocks = block_user.shape[0]
    h, gram, c = fetch(
        n,
        items,
        requests,
        slots.reshape(blocks, -1),
        confidence.reshape(blocks, -1),
        block_user,
        column_block,
    )
    flat, right, message = normals(h, c, counts, light, heavy, column_block)
    heavy_sum = reduce_heavy(lax.axis_size("rep"), message)
    prior = UNOBSERVED / (items.shape[0] * n)
    return solve(prior, flat, right, heavy_sum, gram, light, heavy, column_block)


def solution(mesh):
    both = ("grp", "rep")
    return jax.shard_map(
        local,
        mesh=mesh,
        in_specs=(
            P("grp", None),
            P(both, None),
            P("grp", None),
            P(both, None),
            P(both, None),
            P(both),
            P(both),
            P(both),
            P(),
        ),
        out_specs=(P(both, None), P(both, None)),
        check_vma=False,
    )
```

time: 759 us -> 122 us (0.16)
  waiting for transfers between devices: 298 us -> 0 us
  blocking collectives: 189 us -> 0 us
  other arithmetic: 186 us -> 0 us
  Pallas kernels: 0 us -> 114 us
  local copies, waits for them, and re-layouts: 57.1 us -> 6.03 us
  between operations: 16.5 us -> 1.32 us
  matrix products: 8.56 us -> 0 us
    psum x2 -> x0, waiting for transfers between devices: 297 us -> none  [the longest x1 249 us: local(): item_gram = lax.psum(local_gram, 'grp')]
    another operation x7 -> x0, other arithmetic: 184 us -> none  [the longest x4 99.8 us: refine(): factor = jnp.linalg.cholesky(system)]
    psum x1 -> x0, blocking collectives: 139 us -> none  [local(): total_normal, total_right = lax.psum((heavy_normal, heavy_right), 'rep')]
    pallas_call x0 -> x4, Pallas kernels: none -> 114 us  [the longest x1 93.8 us: fetch(): pl.pallas_call(functools.partial(fetch_kernel, n, items.shape[0] * n), ou...]
    gather x4 -> x0, local copies, waits for them, and re-layouts: 50.7 us -> none  [the longest x1 32.8 us: local(): predicted = score_table[row_owner, slots]]
    all_to_all x1 -> x0, blocking collectives: 50.3 us -> none  [local(): lax.all_to_all(requests, 'grp', split_axis=0, concat_axis=0, tiled=True)]
  transfers between devices with their start and end apart: 3 -> 0, of which waited for: 2 -> 0; matrix products, arithmetic and copies ran while one was open for 1% -> 0% of each run, Pallas kernels for 0% -> 0%
where the time goes in v1:
time: 122 us; the launch traced here: 121 us
  Pallas kernels  114 us (93%)
  local copies, waits for them, and re-layouts  6.03 us (5%)
  between operations  1.32 us (1%)
    pallas_call x1, Pallas kernels, fetch(): pl.pallas_call(functools.partial(fetch_kernel, n, items.shape[0] * n), ou...  93.8 us
    pallas_call x1, Pallas kernels, reduce_heavy(): pl.pallas_call(functools.partial(reduce_kernel, n), out_shape=jax.ShapeDt...  12.7 us
    unnamed x15, local copies, waits for them, and re-layouts  6.03 us
    pallas_call x1, Pallas kernels, solve(): pl.pallas_call(functools.partial(solve_kernel, prior), out_shape=(jax.Sha...  4.66 us
    pallas_call x1, Pallas kernels, normals(): pl.pallas_call(normal_kernel, out_shape=(jax.ShapeDtypeStruct((ENTRIES, 1...  2.75 us

profile of v1, /device:TPU:1, one launch (start us, length us, event | category | flops | bytes accessed | tf_op | source)
XLA Modules:
  0.0 121.3 jit_solution(233858634315680134)
XLA Ops:
  1.3 0.8 copy.11.req_ref
  2.0 0.0 copy-start
  2.0 1.0 copy-done
  3.1 0.0 copy-start.3
  3.1 0.7 copy-done.3
  3.8 0.0 copy-start.4
  3.8 0.7 copy-done.4
  4.5 0.0 copy-start.5
  4.5 0.7 copy-done.5
  5.2 93.8 %fetch.1 = (f32[32,16,256]{2,1,0:T(8,128)S(1)}, f32[64,256]{1,0:T(8,128)S(1)}, f32[48,512]{1,0:T(8,128)S(1)}) custom-call(s32[1]{0:T(128)S(6)} %copy.12.cb_ref, s32[32]{0:T(128)S(1)} %copy-done.5, f32[512,256]{1,0:T(8,128)S(1)} %copy-done, s32[32,16]{1,0:T(8,128)S(1)} %copy.11.req_ref, s32[32,128]{1,0:T(8,128)S(1)} %bitcast.2, f32[32,128]{1,0:T(8,128)S(1)} %bitcast.3), custom_call_target="tpu_custom_call" | custom-call | tf_op jit(solution)/shard_map/fetch/pallas_call | solution.py:275
  99.0 0.0 copy-start.1
  99.0 0.7 copy-done.1
  99.8 0.0 copy-start.2
  99.8 0.7 copy-done.2
  100.5 0.0 copy-start.6
  100.5 0.7 copy-done.6
  101.1 2.8 %normals.1 = (f32[2304,128]{1,0:T(8,128)S(1)}, f32[64,128]{1,0:T(8,128)S(1)}, f32[32,24,128]{2,1,0:T(8,128)S(1)}) custom-call(s32[1]{0:T(128)S(6)} %copy.12.cb_ref, f32[32,16,256]{2,1,0:T(8,128)S(1)} %get-tuple-element.8.h_ref, f32[48,512]{1,0:T(8,128)S(1)} %get-tuple-element.9.c_ref, s32[1,32]{1,0:T(1,128)S(1)} %copy-done.6, f32[16,256]{1,0:T(8,128)S(1)} %copy-done.2, ...), custom_call_target="tpu_custom_call" | custom-call | tf_op jit(solution)/shard_map/normals/pallas_call | solution.py:341
  103.9 12.7 %reduce_heavy.1.heavy_sum_ref = f32[24,128]{1,0:T(8,128)S(1)} custom-call(f32[32,24,128]{2,1,0:T(8,128)S(1)} %get-tuple-element.12.msg_ref), custom_call_target="tpu_custom_call" | custom-call | tf_op jit(solution)/shard_map/reduce_heavy/pallas_call | solution.py:387
  116.7 4.7 %solve.1 = (f32[16,256]{1,0:T(8,128)}, f32[1,256]{1,0:T(1,128)}) custom-call(s32[1]{0:T(128)S(6)} %copy.12.cb_ref, f32[2304,128]{1,0:T(8,128)S(1)} %get-tuple-element.10.flat_ref, f32[64,128]{1,0:T(8,128)S(1)} %get-tuple-element.11.right_ref, f32[24,128]{1,0:T(8,128)S(1)} %reduce_heavy.1.heavy_sum_ref, f32[64,256]{1,0:T(8,128)S(1)} %get-tuple-element.13.gram_ref, ...), custom_call_target="tpu_custom_call" | custom-call | tf_op jit(solution)/shard_map/solve/pallas_call | solution.py:502
Async XLA Ops:
  2.0 1.0 copy-start
  3.1 0.7 copy-start.3
  3.8 0.7 copy-start.4
  4.5 0.7 copy-start.5
  99.0 0.8 copy-start.1
  99.8 0.7 copy-start.2
  100.5 0.7 copy-start.6

commit v2 on v1

v2 whole, which is shorter than its diff:
```python
import functools

import jax
import jax.numpy as jnp
from jax import lax
from jax.experimental import pallas as pl
from jax.experimental.pallas import tpu as pltpu
from jax.sharding import PartitionSpec as P

COLS = 64
RANK = 256
SLOTS = 512
CAP = 16
LIGHT = 16
HEAVY = 32
TILE = 8
PANELS = COLS // TILE
UNOBSERVED = 128.0
MESH = pl.DeviceIdType.MESH
F32 = jnp.float32
BF16 = jnp.bfloat16
HIGHEST = lax.Precision.HIGHEST
VMEM = pl.BlockSpec(memory_space=pltpu.VMEM)
SMEM = pl.BlockSpec(memory_space=pltpu.SMEM)
HBM = pl.BlockSpec(memory_space=pltpu.HBM)
LIMIT = 56 * 1024 * 1024

WIDTH = [COLS - TILE * b for b in range(PANELS)]
START = [sum(TILE * w for w in WIDTH[:b]) for b in range(PANELS)]
ENTRIES = sum(TILE * w for w in WIDTH)
LINES = ENTRIES // 128
MESSAGE = 24

SPINE = [0, 5, 10, 14, -5, -10, -14]
FORWARD = [(1, 0), (4, 0), (2, 1), (5, 4), (3, 2), (6, 5)]
REACH = [0, 5, 10, 14]
LEAVES = [(0, 1, -1, 2, -2)] * 3 + [(2, 1, 0, -1)] + [(0, 1, -1, 2, -2)] * 2 + [(-1, 0, 1)]


def iota(shape, dim):
    return lax.broadcasted_iota(jnp.int32, shape, dim)


def rows_by_rows(a, b, precision=HIGHEST):
    return lax.dot_general(a, b, (((1,), (1,)), ((), ())), precision=precision, preferred_element_type=F32)


def split(x, parts):
    out = []
    for _ in range(parts):
        part = x.astype(BF16)
        out.append(part)
        x = x - part.astype(F32)
    return out


def picker(column_block):
    return (iota((COLS, RANK), 1) == iota((COLS, RANK), 0) + column_block * COLS).astype(F32)


def gather_kernel(
    n,
    cb_ref,
    items_ref,
    req_ref,
    slots_ref,
    conf_ref,
    user_ref,
    counts_ref,
    light_ref,
    heavy_ref,
    flat_out,
    right_ref,
    reduced_ref,
    gram_ref,
    flat_ref,
    heavy_flat,
    load_out,
    load_in,
    sum_out,
    sum_in,
    spine,
    owned,
    answer,
    rows_ref,
    ask_out,
    ask_in,
    part_out,
    part_in,
    msg,
    landed,
    hot_ref,
    by_block,
    req_buf,
    slots_buf,
    conf_buf,
    user_buf,
    counts_buf,
    factors,
    load_sem,
    spine_s,
    spine_r,
    leaf_s,
    own_r,
    ask_s,
    ask_r,
    ans_s,
    ans_r,
    part_s,
    part_r,
    msg_s,
    msg_r,
    load_s,
    load_r,
    sum_s,
    sum_r,
):
    g, r = lax.axis_index("grp"), lax.axis_index("rep")
    share = owned.shape[1]
    users = LIGHT + HEAVY

    def plane(k):
        return lax.rem(g + (k + n), n)

    def put(src, dst, send, recv, target):
        return pltpu.make_async_remote_copy(
            src_ref=src, dst_ref=dst, send_sem=send, recv_sem=recv, device_id=target, device_id_type=MESH
        )

    def peers(body):
        def one(k, carry):
            body(lax.rem(r + k, n))
            return carry

        lax.fori_loop(1, n, one, 0)

    off = lax.rem(g + n - r, n)
    behind = off // (n // 2 + 1)
    size = off + behind * (n - 2 * off)
    level = (size + 2) // 5
    step = 5 * level - level // 3
    source = lax.rem(r + step * (1 - 2 * behind) + n, n)

    barrier = pltpu.get_barrier_semaphore()

    @pl.when(source != g)
    def _():
        def greet(k, carry):
            pl.semaphore_signal(barrier, inc=1, device_id=(source, k), device_id_type=MESH)
            return carry

        lax.fori_loop(0, n, greet, 0)

    for hop in (5, -5, 4, -4):
        pl.semaphore_signal(barrier, inc=1, device_id=(plane(hop), r), device_id_type=MESH)
    peers(lambda p: pl.semaphore_signal(barrier, inc=1, device_id=(g, p), device_id_type=MESH))
    loads = [
        (items_ref.at[pl.ds(pl.multiple_of(r * share, share), share)], spine.at[0]),
        (req_ref, req_buf),
        (slots_ref, slots_buf),
        (conf_ref, conf_buf),
        (user_ref, user_buf),
        (counts_ref, counts_buf),
        (light_ref, factors.at[pl.ds(0, LIGHT)]),
        (heavy_ref, factors.at[pl.ds(LIGHT, HEAVY)]),
    ]
    loads = [pltpu.make_async_copy(src, dst, load_sem.at[k]) for k, (src, dst) in enumerate(loads)]
    for load in loads:
        load.start()

    leaves = [(k, e) for k in range(len(SPINE)) for e in LEAVES[k]]
    loads[1].wait()
    spread = (
        (iota((CAP, 128), 1) % CAP == iota((CAP, 128), 0)) & (iota((CAP, 128), 1) // CAP == lax.rem(r, TILE))
    ).astype(F32)
    asked = lax.dot_general(
        req_buf[...].astype(F32), spread, (((0,), (0,)), ((), ())), precision=HIGHEST, preferred_element_type=F32
    )
    for p in range(n):
        ask_out[p] = asked[p : p + 1, :]
    loads[0].wait()
    pl.semaphore_wait(barrier, n - 1 + 4 + sum(e != 0 for _, e in leaves))

    def ahead(k, from_k):
        hop = SPINE[k] - SPINE[from_k]
        return put(spine.at[from_k], spine.at[k], spine_s.at[k], spine_r.at[k], (plane(hop), r))

    def leaf(index):
        k, e = leaves[index]
        owner = plane(-SPINE[k])
        return owner, put(spine.at[k], owned.at[r], leaf_s.at[index], own_r.at[r], (plane(e), owner))

    def pass_on(k):
        for later, earlier in FORWARD:
            if earlier == k:
                ahead(later, k).start()
        for index, (at, e) in enumerate(leaves):
            if at != k:
                continue
            owner, copy = leaf(index)
            if e != 0:
                copy.start()
                continue

            @pl.when(owner != r)
            def _(copy=copy):
                copy.start()

            @pl.when(owner == r)
            def _():
                owned[r] = spine[k]

    def ask(p):
        return put(ask_out.at[p], ask_in.at[r], ask_s.at[p], ask_r.at[r], (g, p))

    def asked_by(p):
        return put(ask_out.at[p], ask_in.at[p], ask_s.at[p], ask_r.at[p], (g, p))

    pass_on(0)
    peers(lambda p: ask(p).start())
    ask_in[r] = ask_out[r]

    def weigh(step, carry):
        for k in range(4):
            row = 4 * step + k
            slot = slots_buf[pl.ds(row, 1), :]
            parts = [part.astype(F32) for part in split(conf_buf[pl.ds(row, 1), :], 3)]
            place = iota((16, 128), 0)
            parts = jnp.where(
                place < 4, parts[0], jnp.where(place < 8, parts[1], jnp.where(place < 12, parts[2], 0.0))
            )
            lhs = jnp.where((place & 3) == (slot >> 7), parts, 0.0).astype(BF16)
            hot = (iota((128, 128), 0) == (slot & 127)).astype(F32).astype(BF16)
            got = rows_by_rows(lhs, hot, None)
            got = got[0:4] + got[4:8] + got[8:12]
            by_block[pl.ds(row, 1), :] = jnp.concatenate([got[a : a + 1] for a in range(4)], 1)
        return carry

    for load in loads[2:]:
        load.wait()
    lax.fori_loop(0, by_block.shape[0] // 4, weigh, 0)

    peers(lambda p: asked_by(p).wait_recv())
    lines = [jnp.sum(ask_in[TILE * q : TILE * q + TILE], axis=0) for q in range(n // TILE)]
    lines = jnp.concatenate(lines + [jnp.zeros((TILE - len(lines), 128), F32)], 0)
    eye = (iota((128, 128), 0) == iota((128, 128), 1)).astype(F32)
    wanted = rows_by_rows(eye, lines)
    for q in range(n // TILE):
        hot_ref[128 * q : 128 * q + 128, :] = (
            (wanted[:, q : q + 1] == iota((128, SLOTS), 1).astype(F32)).astype(F32).astype(BF16)
        )

    def reply(p):
        return put(answer.at[p], rows_ref.at[r], ans_s.at[p], ans_r.at[r], (g, p))

    def replied_by(p):
        return put(answer.at[p], rows_ref.at[p], ans_s.at[p], ans_r.at[p], (g, p))

    pick = picker(cb_ref[0])

    def give(p):
        return put(part_out.at[p], part_in.at[r], part_s.at[p], part_r.at[r], (g, p))

    def given_by(p):
        return put(part_out.at[p], part_in.at[p], part_s.at[p], part_r.at[p], (g, p))

    def stand_in():
        def arrived(k, carry):
            @pl.when(n * source + k != n * g + r)
            def _():
                put(spine.at[0], owned.at[k], leaf_s.at[0], own_r.at[k], (source, k)).wait_recv()

            return carry

        lax.fori_loop(0, n, arrived, 0)
        parts = split(owned[...].reshape(n * share, RANK), 2)
        half = n // 2

        def block(q, carry):
            at = lax.rem(r // half + 1 + q, 2)
            hot = hot_ref[pl.ds(pl.multiple_of(CAP * half * at, CAP * half), CAP * half), :]
            got = sum(jnp.dot(hot, part, preferred_element_type=F32) for part in parts)
            answer[pl.ds(pl.multiple_of(half * at, half), half)] = got.reshape(half, CAP, RANK)

            def one(k, inner):
                p = half * at + lax.rem(r + k, half)

                @pl.when(p != r)
                def _():
                    reply(p).start()

                @pl.when(p == r)
                def _():
                    rows_ref[r] = answer[r]

                return inner

            return lax.fori_loop(0, half, one, carry)

        lax.fori_loop(0, 2, block, 0)

    def burden(p):
        return put(load_out.at[p], load_in.at[r], load_s.at[p], load_r.at[r], (g, p))

    def burden_of(p):
        return put(load_out.at[p], load_in.at[p], load_s.at[p], load_r.at[p], (g, p))

    for at in range(4):
        if at == 1:
            owners = counts_buf.shape[1]
            by_slot = (iota((owners, SLOTS), 1) // CAP == iota((owners, SLOTS), 0)).astype(F32).astype(BF16)
            limit = jnp.dot(
                jnp.broadcast_to(counts_buf[...], (TILE, owners)).astype(F32).astype(BF16),
                by_slot,
                preferred_element_type=F32,
            )[:1]
            live = (iota((1, SLOTS), 1) % CAP).astype(F32) < limit
            of_user = (iota((users, by_block.shape[0]), 0) == user_buf[...]).astype(F32)
            weight = jnp.dot(of_user, by_block[...], precision=HIGHEST, preferred_element_type=F32)
            weight = jnp.where(live, weight, 0.0)
            light_weight = weight[:LIGHT]
            turned = jnp.concatenate([weight[LIGHT:], jnp.zeros((128 - HEAVY, SLOTS), F32)], 0).T
            load_out[...] = turned.reshape(n, CAP, 128)
            peers(lambda p: burden(p).start())
            load_in[r] = load_out[r]
        if at < 3:
            for later, earlier in FORWARD:
                if abs(SPINE[later]) == REACH[at + 1]:
                    hop = SPINE[later] - SPINE[earlier]
                    put(
                        spine.at[earlier], spine.at[later], spine_s.at[later], spine_r.at[later], (plane(-hop), r)
                    ).wait_recv()
                    pass_on(later)
        if at == 3:
            peers(lambda p: burden_of(p).wait_recv())
            heavy_weight = load_in[...].reshape(n * CAP, 128).T[:HEAVY]
            parts = jnp.concatenate([part.astype(F32) for part in split(heavy_weight, 3)], 0).astype(BF16)
            heavy_weight = jnp.dot(parts, hot_ref[...], preferred_element_type=F32)
            heavy_weight = (
                heavy_weight[:HEAVY] + heavy_weight[HEAVY : 2 * HEAVY] + heavy_weight[2 * HEAVY :]
            )
        pl.when(level == at)(stand_in)

    def sum_of(p):
        return put(sum_out.at[0], sum_in.at[p], sum_s.at[p], sum_r.at[p], (g, p))

    def share_sum(p):
        return put(sum_out.at[0], sum_in.at[r], sum_s.at[p], sum_r.at[r], (g, p))

    def send(p):
        return put(msg.at[p], landed.at[r], msg_s.at[p], msg_r.at[r], (g, p))

    def sent_by(p):
        return put(msg.at[p], landed.at[p], msg_s.at[p], msg_r.at[p], (g, p))

    def normals(into, cols, weight, residual):
        count = weight.shape[0]
        none = jnp.zeros((64 - count, SLOTS), F32)
        high, low = [part.astype(F32) for part in split(weight, 2)]
        both = jnp.concatenate([high, none, low, none], 0).astype(BF16)
        once = jnp.concatenate([high, none, jnp.zeros((64, SLOTS), F32)], 0).astype(BF16)
        for b in range(PANELS):
            width = WIDTH[b]
            tail = cols[TILE * b :]
            product = jnp.concatenate([tail * cols[TILE * b + i : TILE * b + i + 1] for i in range(TILE)], 0)
            p_high, p_low = split(product, 2)
            first = rows_by_rows(p_high, both, None)
            second = rows_by_rows(p_low, once, None)
            into[START[b] : START[b] + TILE * width, :] = first + pltpu.roll(first, 64, 1) + second
        return rows_by_rows(cols, jnp.concatenate([residual, jnp.zeros((128 - count, SLOTS), F32)], 0))

    mine = owned[...].reshape(n * share, RANK)
    cols = rows_by_rows(pick, mine)
    part = jnp.dot(cols, mine, precision=HIGHEST, preferred_element_type=F32)
    for k in range(n):
        a, b, c = k // 4, (k // 2) % 2, k % 2
        part_out[k] = part[8 * a + 4 * c : 8 * a + 4 * c + 4, 128 * b : 128 * b + 128]
    peers(lambda p: give(p).start())
    part_in[r] = part_out[r]

    residual = heavy_weight * (1.0 - rows_by_rows(factors[LIGHT:users, :], mine))
    right = normals(heavy_flat, cols, heavy_weight, residual)
    for q in range(LINES):
        msg[:, q, :] = heavy_flat[128 * q : 128 * q + 128, :].T[:HEAVY]
    msg[:, LINES, :] = jnp.concatenate([right, jnp.zeros((64, 128), F32)], 0).T[:HEAVY]
    for q in range(LINES + 1, MESSAGE):
        msg[:, q, :] = jnp.zeros((HEAVY, 128), F32)
    peers(lambda p: send(p).start())
    landed[r] = msg[r]

    peers(lambda p: given_by(p).wait_recv())
    sum_out[0] = jnp.sum(part_in[...], axis=0)
    peers(lambda p: share_sum(p).start())
    sum_in[r] = sum_out[0]

    peers(lambda p: replied_by(p).wait_recv())
    rows = rows_ref[...].reshape(SLOTS, RANK)
    residual = light_weight * (1.0 - rows_by_rows(factors[:LIGHT, :], rows))
    right_ref[...] = normals(flat_ref, rows_by_rows(pick, rows), light_weight, residual)
    keep = pltpu.make_async_copy(flat_ref, flat_out, load_sem.at[0])
    keep.start()

    for later, earlier in FORWARD:
        ahead(later, earlier).wait_send()
    for index, (at, e) in enumerate(leaves):
        owner, copy = leaf(index)
        if e != 0:
            copy.wait_send()
        else:
            pl.when(owner != r)(copy.wait_send)
    for sent in (ask, reply, give, burden, share_sum):
        peers(lambda p, sent=sent: sent(p).wait_send())

    peers(lambda p: sent_by(p).wait_recv())
    reduced_ref[...] = jnp.sum(landed[...], axis=0)
    peers(lambda p: sum_of(p).wait_recv())
    for k in range(n):
        a, b, c = k // 4, (k // 2) % 2, k % 2
        gram_ref[8 * a + 4 * c : 8 * a + 4 * c + 4, 128 * b : 128 * b + 128] = sum_in[k]
    peers(lambda p: send(p).wait_send())
    keep.wait()


def gather(n, items, requests, slots, confidence, block_user, counts, light, heavy, column_block):
    share = items.shape[0] // n
    blocks = slots.shape[0]
    users = LIGHT + HEAVY
    dma = [pltpu.SemaphoreType.DMA((n,)) for _ in range(14)]
    return pl.pallas_call(
        functools.partial(gather_kernel, n),
        out_shape=(
            jax.ShapeDtypeStruct((ENTRIES, 128), F32),
            jax.ShapeDtypeStruct((COLS, 128), F32),
            jax.ShapeDtypeStruct((MESSAGE, 128), F32),
            jax.ShapeDtypeStruct((COLS, RANK), F32),
        ),
        in_specs=[SMEM] + [HBM] * 8,
        out_specs=(HBM, VMEM, VMEM, VMEM),
        scratch_shapes=[
            pltpu.VMEM((ENTRIES, 128), F32),
            pltpu.VMEM((ENTRIES, 128), F32),
            pltpu.VMEM((n, CAP, 128), F32),
            pltpu.VMEM((n, CAP, 128), F32),
            pltpu.VMEM((1, 4, 128), F32),
            pltpu.VMEM((n, 4, 128), F32),
            pltpu.VMEM((len(SPINE), share, RANK), F32),
            pltpu.VMEM((n, share, RANK), F32),
            pltpu.VMEM((n, CAP, RANK), F32),
            pltpu.VMEM((n, CAP, RANK), F32),
            pltpu.VMEM((n, 1, 128), F32),
            pltpu.VMEM((n, 1, 128), F32),
            pltpu.VMEM((n, 4, 128), F32),
            pltpu.VMEM((n, 4, 128), F32),
            pltpu.VMEM((n, MESSAGE, 128), F32),
            pltpu.VMEM((n, MESSAGE, 128), F32),
            pltpu.VMEM((n * CAP, SLOTS), BF16),
            pltpu.VMEM((blocks, SLOTS), F32),
            pltpu.VMEM(requests.shape, jnp.int32),
            pltpu.VMEM(slots.shape, jnp.int32),
            pltpu.VMEM(slots.shape, F32),
            pltpu.VMEM((1, blocks), jnp.int32),
            pltpu.VMEM(counts.shape, jnp.int32),
            pltpu.VMEM((users, RANK), F32),
            pltpu.SemaphoreType.DMA((8,)),
            pltpu.SemaphoreType.DMA((len(SPINE),)),
            pltpu.SemaphoreType.DMA((len(SPINE),)),
            *dma,
        ],
        compiler_params=pltpu.CompilerParams(collective_id=0, has_side_effects=True, vmem_limit_bytes=LIMIT),
        name="gather",
    )(column_block, items, requests, slots, confidence, block_user, counts, light, heavy)


def solve_kernel(
    prior,
    cb_ref,
    flat_in,
    right_ref,
    heavy_sum_ref,
    gram_ref,
    light_ref,
    heavy_ref,
    light_out,
    heavy_out,
    flat_ref,
    flat_sem,
    a_ref,
    l_ref,
    inv_ref,
    x_ref,
):
    flat_load = pltpu.make_async_copy(flat_in, flat_ref, flat_sem)
    flat_load.start()
    r = lax.axis_index("rep")
    pick = picker(cb_ref[0])
    own = heavy_ref[pl.ds(r, 1), :]
    factors = jnp.concatenate([light_ref[...], own, jnp.zeros((128 - LIGHT - 1, RANK), F32)], 0)
    gram = prior * gram_ref[...]
    block = rows_by_rows(gram, pick) + (iota((COLS, COLS), 0) == iota((COLS, COLS), 1)).astype(F32)
    pulled = rows_by_rows(gram + pick, factors)
    turned = jnp.concatenate([heavy_sum_ref[...], jnp.zeros((128 - MESSAGE, 128), F32)], 0).T
    lane = iota((1, 128), 1)
    is_light, is_heavy = lane < LIGHT, lane == LIGHT
    right = jnp.where(is_light, right_ref[...], jnp.where(is_heavy, turned[:COLS, LINES : LINES + 1], 0.0)) - pulled
    flat_load.wait()
    for q in range(LINES):
        part = flat_ref[128 * q : 128 * q + 128, :]
        flat_ref[128 * q : 128 * q + 128, :] = jnp.where(
            is_light, part, jnp.where(is_heavy, turned[:, q : q + 1], 0.0)
        )
    for i in range(COLS):
        b = i // TILE
        at = START[b] + (i - TILE * b) * WIDTH[b]
        a_ref[i, TILE * b : COLS, :] = flat_ref[at : at + WIDTH[b], :] + block[TILE * b :, i : i + 1]
        a_ref[i, COLS : COLS + TILE, :] = jnp.broadcast_to(right[i : i + 1, :], (TILE, 128))

    tiles = PANELS + 1
    for b in range(PANELS):
        base = TILE * b
        acc = {
            (k, t): a_ref[base + k, TILE * t : TILE * t + TILE, :] for k in range(TILE) for t in range(b, tiles)
        }
        for k in range(TILE):
            own_tile = acc[k, b]
            inv = 1.0 / jnp.broadcast_to(own_tile[k : k + 1], (TILE, 128))
            inv_ref[base + k] = inv
            for t in range(b, tiles):
                if t > b:
                    a_ref[base + k, TILE * t : TILE * t + TILE, :] = acc[k, t]
                    if t < PANELS:
                        l_ref[base + k, TILE * t : TILE * t + TILE, :] = acc[k, t] * inv
            a_ref[base + k, base : base + TILE, :] = own_tile
            for k2 in range(k + 1, TILE):
                factor = jnp.broadcast_to(own_tile[k2 : k2 + 1], (TILE, 128)) * inv
                for t in range(b, tiles):
                    acc[k2, t] = acc[k2, t] - factor * acc[k, t]
        for s in range(b + 1, PANELS):
            for k2 in range(TILE):
                row = TILE * s + k2
                factors_ = [
                    jnp.broadcast_to(l_ref[base + k, row : row + 1, :], (TILE, 128)) for k in range(TILE)
                ]
                for t in range(s, tiles):
                    total = a_ref[row, TILE * t : TILE * t + TILE, :]
                    for k in range(TILE):
                        total = total - factors_[k] * a_ref[base + k, TILE * t : TILE * t + TILE, :]
                    a_ref[row, TILE * t : TILE * t + TILE, :] = total

    x = [None] * PANELS
    place = iota((TILE, 128), 0)
    for b in reversed(range(PANELS)):
        base = TILE * b
        left = []
        for k in range(TILE):
            value = a_ref[base + k, COLS : COLS + TILE, :]
            if b + 1 < PANELS:
                total = sum(
                    a_ref[base + k, TILE * t : TILE * t + TILE, :] * x[t] for t in range(b + 1, PANELS)
                )
                value = value - jnp.sum(total, axis=0, keepdims=True)
            left.append(value)
        found = jnp.zeros((TILE, 128), F32)
        for k in reversed(range(TILE)):
            value = left[k] * inv_ref[base + k]
            found = jnp.where(place == k, value, found)
            for k2 in range(k):
                left[k2] = left[k2] - jnp.broadcast_to(a_ref[base + k2, base + k : base + k + 1, :], (TILE, 128)) * value
        x[b] = found
        x_ref[base : base + TILE, :] = found
    x_ref[COLS:, :] = jnp.zeros((128 - COLS, 128), F32)
    delta = x_ref[...].T[:, :COLS]
    delta = jnp.concatenate([delta, delta, delta, delta], 1)
    inside = iota((1, RANK), 1) // COLS == cb_ref[0]
    light_out[...] = light_ref[...] + jnp.where(inside, delta[:LIGHT], 0.0)
    heavy_out[...] = own + jnp.where(inside, delta[LIGHT : LIGHT + 1], 0.0)


def solve(prior, flat, right, heavy_sum, gram, light, heavy, column_block):
    return pl.pallas_call(
        functools.partial(solve_kernel, prior),
        out_shape=(jax.ShapeDtypeStruct((LIGHT, RANK), F32), jax.ShapeDtypeStruct((1, RANK), F32)),
        in_specs=[SMEM, HBM, VMEM, VMEM, VMEM, VMEM, VMEM],
        out_specs=(VMEM, VMEM),
        scratch_shapes=[
            pltpu.VMEM((ENTRIES, 128), F32),
            pltpu.SemaphoreType.DMA(()),
            pltpu.VMEM((COLS, COLS + TILE, 128), F32),
            pltpu.VMEM((COLS, COLS, 128), F32),
            pltpu.VMEM((COLS, TILE, 128), F32),
            pltpu.VMEM((128, 128), F32),
        ],
        compiler_params=pltpu.CompilerParams(vmem_limit_bytes=LIMIT),
        name="solve",
    )(column_block, flat, right, heavy_sum, gram, light, heavy)


def local(items, light, heavy, requests, counts, slots, confidence, block_user, column_block):
    n = lax.axis_size("grp")
    blocks = block_user.shape[0]
    flat, right, heavy_sum, gram = gather(
        n,
        items,
        requests.T,
        slots.reshape(blocks, -1),
        confidence.reshape(blocks, -1),
        block_user.reshape(1, blocks),
        counts,
        light,
        heavy,
        column_block,
    )
    prior = UNOBSERVED / (items.shape[0] * n)
    return solve(prior, flat, right, heavy_sum, gram, light, heavy, column_block)


def solution(mesh):
    both = ("grp", "rep")
    return jax.shard_map(
        local,
        mesh=mesh,
        in_specs=(
            P("grp", None),
            P(both, None),
            P("grp", None),
            P(both, None),
            P(both, None),
            P(both),
            P(both),
            P(both),
            P(),
        ),
        out_specs=(P(both, None), P(both, None)),
        check_vma=False,
    )
```

time: 122 us -> 80.5 us (0.66)
  Pallas kernels: 114 us -> 78.9 us
  local copies, waits for them, and re-layouts: 6.03 us -> 0 us
    pallas_call x3 -> x1, Pallas kernels: 109 us -> 72.5 us  [gather(): pl.pallas_call(functools.partial(gather_kernel, n), out_shape=(jax.ShapeD...]
    unnamed x15 -> x0, local copies, waits for them, and re-layouts: 6.03 us -> none
    pallas_call x1, Pallas kernels: 4.66 us -> 6.38 us  [solve(): pl.pallas_call(functools.partial(solve_kernel, prior), out_shape=(jax.Sha...]
where the time goes in v2:
time: 80.5 us; the launch traced here: 80.2 us
  Pallas kernels  78.9 us (98%)
  between operations  1.29 us (2%)
    pallas_call x1, Pallas kernels, gather(): pl.pallas_call(functools.partial(gather_kernel, n), out_shape=(jax.ShapeD...  72.5 us
    pallas_call x1, Pallas kernels, solve(): pl.pallas_call(functools.partial(solve_kernel, prior), out_shape=(jax.Sha...  6.38 us

profile of v2, /device:TPU:1, one launch (start us, length us, event | category | flops | bytes accessed | tf_op | source)
XLA Modules:
  0.0 80.2 jit_solution(9759091648907330069)
XLA Ops:
  1.3 72.5 %gather.1 = (f32[2304,128]{1,0:T(8,128)}, f32[64,128]{1,0:T(8,128)}, f32[24,128]{1,0:T(8,128)}, f32[64,256]{1,0:T(8,128)}) custom-call(s32[1]{0:T(128)S(6)} %copy.11.cb_ref, f32[512,256]{1,0:T(8,128)} %items_ref.1, s32[16,32]{1,0:T(8,128)} %bitcast.6, s32[32,128]{1,0:T(8,128)} %bitcast.4, f32[32,128]{1,0:T(8,128)} %bitcast.5, s32[1,32]{1,0:T(1,128)} %bitcast.7, ...), custom_call_target="tpu_custom_call" | custom-call | tf_op jit(solution)/shard_map/gather/pallas_call | solution.py:429
  73.8 6.4 %solve.1 = (f32[16,256]{1,0:T(8,128)}, f32[1,256]{1,0:T(1,128)}) custom-call(s32[1]{0:T(128)S(6)} %copy.11.cb_ref, f32[2304,128]{1,0:T(8,128)} %get-tuple-element.6.flat_in, f32[64,128]{1,0:T(8,128)} %get-tuple-element.7.right_ref, f32[24,128]{1,0:T(8,128)} %get-tuple-element.8.heavy_sum_ref, f32[64,256]{1,0:T(8,128)} %get-tuple-element.9.gram_ref, ...), custom_call_target="tpu_custom_call" | custom-call | tf_op jit(solution)/shard_map/solve/pallas_call | solution.py:579

commit v3 on v2

--- a/solution.py
+++ b/solution.py
@@ -31,10 +31,10 @@
 LINES = ENTRIES // 128
 MESSAGE = 24
 
-SPINE = [0, 5, 10, 14, -5, -10, -14]
-FORWARD = [(1, 0), (4, 0), (2, 1), (5, 4), (3, 2), (6, 5)]
-REACH = [0, 5, 10, 14]
-LEAVES = [(0, 1, -1, 2, -2)] * 3 + [(2, 1, 0, -1)] + [(0, 1, -1, 2, -2)] * 2 + [(-1, 0, 1)]
+SPINE = [0, 7, 14, -7, -14]
+FORWARD = [(1, 0), (3, 0), (2, 1), (4, 3)]
+REACH = [0, 7, 14]
+LEAVES = [(0, 1, -1, 2, -2, 3, -3)] * 2 + [(2, -3, 1, -2, 0, -1)] + [(0, 1, -1, 2, -2, 3, -3), (3, -1, 2, 0, 1)]
 
 
 def iota(shape, dim):
@@ -137,8 +137,8 @@
     off = lax.rem(g + n - r, n)
     behind = off // (n // 2 + 1)
     size = off + behind * (n - 2 * off)
-    level = (size + 2) // 5
-    step = 5 * level - level // 3
+    level = (size + 3) // 7
+    step = 7 * level
     source = lax.rem(r + step * (1 - 2 * behind) + n, n)
 
     barrier = pltpu.get_barrier_semaphore()
@@ -151,7 +151,7 @@
 
         lax.fori_loop(0, n, greet, 0)
 
-    for hop in (5, -5, 4, -4):
+    for hop in (7, -7):
         pl.semaphore_signal(barrier, inc=1, device_id=(plane(hop), r), device_id_type=MESH)
     peers(lambda p: pl.semaphore_signal(barrier, inc=1, device_id=(g, p), device_id_type=MESH))
     loads = [
@@ -179,7 +179,7 @@
     for p in range(n):
         ask_out[p] = asked[p : p + 1, :]
     loads[0].wait()
-    pl.semaphore_wait(barrier, n - 1 + 4 + sum(e != 0 for _, e in leaves))
+    pl.semaphore_wait(barrier, n - 1 + 2 + sum(e != 0 for _, e in leaves))
 
     def ahead(k, from_k):
         hop = SPINE[k] - SPINE[from_k]
@@ -188,7 +188,7 @@
     def leaf(index):
         k, e = leaves[index]
         owner = plane(-SPINE[k])
-        return owner, put(spine.at[k], owned.at[r], leaf_s.at[index], own_r.at[r], (plane(e), owner))
+        return owner, put(spine.at[k], owned.at[r], leaf_s.at[0], own_r.at[0], (plane(e), owner))
 
     def pass_on(k):
         for later, earlier in FORWARD:
@@ -211,10 +211,10 @@
                 owned[r] = spine[k]
 
     def ask(p):
-        return put(ask_out.at[p], ask_in.at[r], ask_s.at[p], ask_r.at[r], (g, p))
-
-    def asked_by(p):
-        return put(ask_out.at[p], ask_in.at[p], ask_s.at[p], ask_r.at[p], (g, p))
+        return put(ask_out.at[p], ask_in.at[r], ask_s.at[0], ask_r.at[0], (g, p))
+
+    def all_asks():
+        return put(ask_out.at[pl.ds(0, n - 1)], ask_in.at[pl.ds(0, n - 1)], ask_s.at[0], ask_r.at[0], (g, lax.rem(r + 1, n)))
 
     pass_on(0)
     peers(lambda p: ask(p).start())
@@ -240,7 +240,7 @@
         load.wait()
     lax.fori_loop(0, by_block.shape[0] // 4, weigh, 0)
 
-    peers(lambda p: asked_by(p).wait_recv())
+    all_asks().wait_recv()
     lines = [jnp.sum(ask_in[TILE * q : TILE * q + TILE], axis=0) for q in range(n // TILE)]
     lines = jnp.concatenate(lines + [jnp.zeros((TILE - len(lines), 128), F32)], 0)
     eye = (iota((128, 128), 0) == iota((128, 128), 1)).astype(F32)
@@ -251,28 +251,28 @@
         )
 
     def reply(p):
-        return put(answer.at[p], rows_ref.at[r], ans_s.at[p], ans_r.at[r], (g, p))
-
-    def replied_by(p):
-        return put(answer.at[p], rows_ref.at[p], ans_s.at[p], ans_r.at[p], (g, p))
+        return put(answer.at[p], rows_ref.at[r], ans_s.at[0], ans_r.at[0], (g, p))
+
+    def all_replies():
+        return put(answer.at[pl.ds(0, n - 1)], rows_ref.at[pl.ds(0, n - 1)], ans_s.at[0], ans_r.at[0], (g, lax.rem(r + 1, n)))
 
     pick = picker(cb_ref[0])
 
     def give(p):
-        return put(part_out.at[p], part_in.at[r], part_s.at[p], part_r.at[r], (g, p))
-
-    def given_by(p):
-        return put(part_out.at[p], part_in.at[p], part_s.at[p], part_r.at[p], (g, p))
+        return put(part_out.at[p], part_in.at[r], part_s.at[0], part_r.at[0], (g, p))
+
+    def all_parts():
+        return put(part_out.at[pl.ds(0, n - 1)], part_in.at[pl.ds(0, n - 1)], part_s.at[0], part_r.at[0], (g, lax.rem(r + 1, n)))
 
     def stand_in():
-        def arrived(k, carry):
-            @pl.when(n * source + k != n * g + r)
-            def _():
-                put(spine.at[0], owned.at[k], leaf_s.at[0], own_r.at[k], (source, k)).wait_recv()
-
-            return carry
-
-        lax.fori_loop(0, n, arrived, 0)
+        @pl.when(source == g)
+        def _():
+            put(owned.at[pl.ds(0, n - 1)], owned.at[pl.ds(0, n - 1)], leaf_s.at[0], own_r.at[0], (plane(1), r)).wait_recv()
+
+        @pl.when(source != g)
+        def _():
+            put(owned, owned, leaf_s.at[0], own_r.at[0], (plane(1), r)).wait_recv()
+
         parts = split(owned[...].reshape(n * share, RANK), 2)
         half = n // 2
 
@@ -300,12 +300,12 @@
         lax.fori_loop(0, 2, block, 0)
 
     def burden(p):
-        return put(load_out.at[p], load_in.at[r], load_s.at[p], load_r.at[r], (g, p))
-
-    def burden_of(p):
-        return put(load_out.at[p], load_in.at[p], load_s.at[p], load_r.at[p], (g, p))
-
-    for at in range(4):
+        return put(load_out.at[p], load_in.at[r], load_s.at[0], load_r.at[0], (g, p))
+
+    def all_burdens():
+        return put(load_out.at[pl.ds(0, n - 1)], load_in.at[pl.ds(0, n - 1)], load_s.at[0], load_r.at[0], (g, lax.rem(r + 1, n)))
+
+    for at in range(3):
         if at == 1:
             owners = counts_buf.shape[1]
             by_slot = (iota((owners, SLOTS), 1) // CAP == iota((owners, SLOTS), 0)).astype(F32).astype(BF16)
@@ -323,7 +323,7 @@
             load_out[...] = turned.reshape(n, CAP, 128)
             peers(lambda p: burden(p).start())
             load_in[r] = load_out[r]
-        if at < 3:
+        if at < 2:
             for later, earlier in FORWARD:
                 if abs(SPINE[later]) == REACH[at + 1]:
                     hop = SPINE[later] - SPINE[earlier]
@@ -331,8 +331,8 @@
                         spine.at[earlier], spine.at[later], spine_s.at[later], spine_r.at[later], (plane(-hop), r)
                     ).wait_recv()
                     pass_on(later)
-        if at == 3:
-            peers(lambda p: burden_of(p).wait_recv())
+        if at == 2:
+            all_burdens().wait_recv()
             heavy_weight = load_in[...].reshape(n * CAP, 128).T[:HEAVY]
             parts = jnp.concatenate([part.astype(F32) for part in split(heavy_weight, 3)], 0).astype(BF16)
             heavy_weight = jnp.dot(parts, hot_ref[...], preferred_element_type=F32)
@@ -341,17 +341,17 @@
             )
         pl.when(level == at)(stand_in)
 
-    def sum_of(p):
-        return put(sum_out.at[0], sum_in.at[p], sum_s.at[p], sum_r.at[p], (g, p))
+    def all_sums():
+        return put(sum_in.at[pl.ds(0, n - 1)], sum_in.at[pl.ds(0, n - 1)], sum_s.at[0], sum_r.at[0], (g, lax.rem(r + 1, n)))
 
     def share_sum(p):
-        return put(sum_out.at[0], sum_in.at[r], sum_s.at[p], sum_r.at[r], (g, p))
+        return put(sum_out.at[0], sum_in.at[r], sum_s.at[0], sum_r.at[0], (g, p))
 
     def send(p):
-        return put(msg.at[p], landed.at[r], msg_s.at[p], msg_r.at[r], (g, p))
-
-    def sent_by(p):
-        return put(msg.at[p], landed.at[p], msg_s.at[p], msg_r.at[p], (g, p))
+        return put(msg.at[p], landed.at[r], msg_s.at[0], msg_r.at[0], (g, p))
+
+    def all_messages():
+        return put(msg.at[pl.ds(0, n - 1)], landed.at[pl.ds(0, n - 1)], msg_s.at[0], msg_r.at[0], (g, lax.rem(r + 1, n)))
 
     def normals(into, cols, weight, residual):
         count = weight.shape[0]
@@ -388,12 +388,12 @@
     peers(lambda p: send(p).start())
     landed[r] = msg[r]
 
-    peers(lambda p: given_by(p).wait_recv())
+    all_parts().wait_recv()
     sum_out[0] = jnp.sum(part_in[...], axis=0)
     peers(lambda p: share_sum(p).start())
     sum_in[r] = sum_out[0]
 
-    peers(lambda p: replied_by(p).wait_recv())
+    all_replies().wait_recv()
     rows = rows_ref[...].reshape(SLOTS, RANK)
     residual = light_weight * (1.0 - rows_by_rows(factors[:LIGHT, :], rows))
     right_ref[...] = normals(flat_ref, rows_by_rows(pick, rows), light_weight, residual)
@@ -402,22 +402,24 @@
 
     for later, earlier in FORWARD:
         ahead(later, earlier).wait_send()
-    for index, (at, e) in enumerate(leaves):
-        owner, copy = leaf(index)
-        if e != 0:
-            copy.wait_send()
-        else:
-            pl.when(owner != r)(copy.wait_send)
-    for sent in (ask, reply, give, burden, share_sum):
-        peers(lambda p, sent=sent: sent(p).wait_send())
-
-    peers(lambda p: sent_by(p).wait_recv())
+    @pl.when(source == g)
+    def _():
+        put(owned.at[pl.ds(0, n - 1)], owned.at[pl.ds(0, n - 1)], leaf_s.at[0], own_r.at[0], (plane(1), r)).wait_send()
+
+    @pl.when(source != g)
+    def _():
+        put(owned, owned, leaf_s.at[0], own_r.at[0], (plane(1), r)).wait_send()
+
+    for sent in (all_asks, all_replies, all_parts, all_burdens, all_sums):
+        sent().wait_send()
+
+    all_messages().wait_recv()
     reduced_ref[...] = jnp.sum(landed[...], axis=0)
-    peers(lambda p: sum_of(p).wait_recv())
+    all_sums().wait_recv()
     for k in range(n):
         a, b, c = k // 4, (k // 2) % 2, k % 2
         gram_ref[8 * a + 4 * c : 8 * a + 4 * c + 4, 128 * b : 128 * b + 128] = sum_in[k]
-    peers(lambda p: send(p).wait_send())
+    all_messages().wait_send()
     keep.wait()
 
 

time: 80.5 us -> 77.5 us (0.963)
  Pallas kernels: 78.9 us -> 75.9 us
    pallas_call x1, Pallas kernels: 72.5 us -> 69.5 us  [gather(): pl.pallas_call(functools.partial(gather_kernel, n), out_shape=(jax.ShapeD...]
where the time goes in v3:
time: 77.5 us; the launch traced here: 77.2 us
  Pallas kernels  75.9 us (98%)
  between operations  1.29 us (2%)
    pallas_call x1, Pallas kernels, gather(): pl.pallas_call(functools.partial(gather_kernel, n), out_shape=(jax.ShapeD...  69.5 us
    pallas_call x1, Pallas kernels, solve(): pl.pallas_call(functools.partial(solve_kernel, prior), out_shape=(jax.Sha...  6.38 us

profile of v3, /device:TPU:1, one launch (start us, length us, event | category | flops | bytes accessed | tf_op | source)
XLA Modules:
  0.0 77.2 jit_solution(17215139544320591190)
XLA Ops:
  1.3 69.5 %gather.1 = (f32[2304,128]{1,0:T(8,128)}, f32[64,128]{1,0:T(8,128)}, f32[24,128]{1,0:T(8,128)}, f32[64,256]{1,0:T(8,128)}) custom-call(s32[1]{0:T(128)S(6)} %copy.11.cb_ref, f32[512,256]{1,0:T(8,128)} %items_ref.1, s32[16,32]{1,0:T(8,128)} %bitcast.6, s32[32,128]{1,0:T(8,128)} %bitcast.4, f32[32,128]{1,0:T(8,128)} %bitcast.5, s32[1,32]{1,0:T(1,128)} %bitcast.7, ...), custom_call_target="tpu_custom_call" | custom-call | tf_op jit(solution)/shard_map/gather/pallas_call | solution.py:431
  70.8 6.4 %solve.1 = (f32[16,256]{1,0:T(8,128)}, f32[1,256]{1,0:T(1,128)}) custom-call(s32[1]{0:T(128)S(6)} %copy.11.cb_ref, f32[2304,128]{1,0:T(8,128)} %get-tuple-element.6.flat_in, f32[64,128]{1,0:T(8,128)} %get-tuple-element.7.right_ref, f32[24,128]{1,0:T(8,128)} %get-tuple-element.8.heavy_sum_ref, f32[64,256]{1,0:T(8,128)} %get-tuple-element.9.gram_ref, ...), custom_call_target="tpu_custom_call" | custom-call | tf_op jit(solution)/shard_map/solve/pallas_call | solution.py:581
